TPU v7x, 32 devices: a whole 2x2x4 slice. The times are simulated.
32 devices in a mesh: ctx: 32 (over z, y, x, core), head: 1.
Axes of the slice: x: 2, y: 2, z: 4, core: 2. Of those that a mesh axis runs over, the one named last changes fastest.
Arguments:
- queries: bfloat16 [4096, 4096], P(('ctx', 'head')), may hold values from -5 to 5
- key_states: bfloat16 [4096, 512], P('ctx', 'head'), may hold values from -5 to 5
- value_states: bfloat16 [4096, 512], P('ctx', 'head'), may hold values from -6 to 6
- outputs: bfloat16 [4096, 4096], P(('ctx', 'head')), may hold values from -6 to 6
- out_grad: bfloat16 [4096, 4096], P(('ctx', 'head')), may hold values from -6 to 6
- doc_of_tile: int32 [32], replicated, may hold values from 0 to 3, never falling along the last dimension, each value on 1 to 16 neighbouring positions
- tile_position: int32 [32], replicated, may hold values from 0 to 31, each once
Outputs:
- query_grad: bfloat16 [4096, 4096], P('ctx', 'head')
- key_grad: bfloat16 [4096, 512], P('ctx', 'head')
- value_grad: bfloat16 [4096, 512], P('ctx', 'head')
Inputs may be any that keep to these rules, and one draw needn't show every extreme that they name: `doc_of_tile`: each document is a run of whole tiles in sequence order, 1 to 16 tiles long, one exactly 16. `tile_position`: a permutation of the 32 sequence tiles.
All inputs are finite; a program needn't handle non-finite values.
Results may differ from a plain program's by a relative error of at most 0.005.
Values may be sent and summed in bfloat16 or wider, within the bound.
A program may use at most 64 MiB of HBM per device.

v0:
```python
import functools

import jax
import jax.numpy as jnp
from jax import lax
from jax.experimental import pallas as pl
from jax.experimental.pallas import tpu as pltpu
from jax.sharding import PartitionSpec as P

HD = 128
TILE = 128
SPAN = 2
LOW = -1e30
LOG2E = 1.4426950408889634
DEEP = 4
SUB = 2
FINE = 4
FLIGHT = 2
GIVE_LIMIT = 52 * 1024 * 1024
ATTENTION_LIMIT = 56 * 1024 * 1024
MESH = pl.DeviceIdType.MESH


def attention_kernel(
    heads,
    tiles,
    team,
    position_ref,
    doc_ref,
    q_hbm,
    g_hbm,
    delta_hbm,
    kv_hbm,
    dq_ref,
    dkv_ref,
    start_ref,
    item_tile,
    item_first,
    item_bound,
    q_rows,
    g_rows,
    q_cols,
    g_cols,
    delta_ref,
    kv_ref,
    gap_ref,
    scores_a,
    scores_b,
    low_a,
    low_b,
    grad_a,
    grad_b,
    probs_buf,
    top_buf,
    top_ref,
    total_ref,
    share_ref,
    dq_acc,
    dkv_acc,
    dq_own,
    dkv_own,
    sems,
):
    width = heads * HD
    scale = HD ** (-0.5)
    pair = SPAN * TILE
    count = position_ref.shape[0]
    block = lax.axis_index("ctx") // team

    def tile_at(index):
        return pl.ds(pl.multiple_of(index * TILE, TILE), TILE)

    heads_in = []
    for h in range(heads):
        lanes = slice(h * HD, (h + 1) * HD)
        for which, (src, dst) in enumerate(((q_hbm, q_rows), (g_hbm, g_rows))):
            copy = pltpu.make_async_copy(
                src.at[:, :, lanes], dst.at[0:tiles, h], sems.at[2 + 2 * h + which]
            )
            copy.start()
            heads_in.append(copy)
    delta_in = pltpu.make_async_copy(delta_hbm, delta_ref.at[0:tiles], sems.at[0])
    delta_in.start()

    @pl.loop(0, count)
    def _(spot):
        place = position_ref[spot]
        for which in range(2):
            pltpu.make_async_copy(
                kv_hbm.at[which, tile_at(spot), :],
                kv_ref.at[which, tile_at(place), :],
                sems.at[1],
            ).start()

    def find(index, start):
        fresh = doc_ref[index] != doc_ref[jnp.maximum(index - 1, 0)]
        start = jnp.where(fresh, index, start)
        start_ref[index] = start
        return start

    lax.fori_loop(0, count, find, jnp.int32(0))

    def put(index, tile, first, bound):
        item_tile[index] = tile
        item_first[index] = first
        item_bound[index] = bound

    def listed(tile, total):
        place = position_ref[block * tiles + tile]
        start = start_ref[place]
        pieces = (place - start + 2) // 2

        @pl.loop(0, pieces)
        def _(step):
            first = start + 2 * step
            put(total + step, tile, first, (place - first) * TILE)

        return total + pieces

    items = lax.fori_loop(0, tiles, listed, jnp.int32(0))
    for extra in range(4):
        put(items + extra, tiles, 0, pair)

    gap_ref[...] = lax.broadcasted_iota(jnp.int32, (pair, TILE), 0) - lax.broadcasted_iota(
        jnp.int32, (pair, TILE), 1
    )
    dkv_acc[...] = jnp.zeros_like(dkv_acc)
    dq_acc[...] = jnp.zeros_like(dq_acc)
    top_ref[...] = jnp.full_like(top_ref, LOW)
    total_ref[...] = jnp.zeros_like(total_ref)
    q_cols[tiles] = jnp.zeros((HD, width), jnp.bfloat16)
    g_cols[tiles] = jnp.zeros((HD, width), jnp.bfloat16)
    q_rows[tiles] = jnp.zeros((heads, TILE, HD), jnp.bfloat16)
    g_rows[tiles] = jnp.zeros((heads, TILE, HD), jnp.bfloat16)
    delta_ref[tiles] = jnp.zeros((8, width), jnp.float32)
    kv_ref[:, count * TILE :, :] = jnp.zeros((2, TILE, HD), jnp.bfloat16)
    low_b[...] = jnp.zeros_like(low_b)
    grad_b[...] = jnp.zeros_like(grad_b)

    for copy in heads_in:
        copy.wait()

    @pl.loop(0, tiles)
    def _(tile):
        for h in range(heads):
            lanes = slice(h * HD, (h + 1) * HD)
            q_cols[tile, :, lanes] = q_rows[tile, h].T
            g_cols[tile, :, lanes] = g_rows[tile, h].T

    delta_in.wait()
    pltpu.make_async_copy(kv_hbm, kv_ref.at[:, 0 : count * TILE], sems.at[1]).wait()

    def groups(value):
        return value.reshape(value.shape[0] // 8, 8, width)

    def area(index):
        return pl.ds(pl.multiple_of(item_first[index] * TILE, TILE), pair)

    def score(index, into):
        into[...] = jnp.dot(
            kv_ref[0, area(index), :],
            q_cols[item_tile[index]],
            preferred_element_type=jnp.float32,
        )

    def weigh(index, source):
        tile = item_tile[index]
        gap = jnp.concatenate([gap_ref[...]] * heads, axis=1)
        scores = groups(
            jnp.where(gap <= item_bound[index], source[...] * (scale * LOG2E), LOW)
        )
        old = top_ref[tile]
        top = jnp.maximum(old, jnp.max(scores, axis=0))
        probs = jnp.exp2(scores - top[None])
        probs_buf[index] = probs.reshape(pair, width)
        top_buf[index] = top
        top_ref[tile] = top
        total_ref[tile] = total_ref[tile] * jnp.exp2(old - top) + jnp.sum(probs, axis=0)

    score(0, scores_a)

    def weigh_two(index):
        score(index + 1, scores_b)
        weigh(index, scores_a)
        score(index + 2, scores_a)
        weigh(index + 1, scores_b)

    rounds = (items + 1) // 2

    @pl.loop(0, rounds // DEEP)
    def _(step):
        for part in range(DEEP):
            weigh_two(2 * (DEEP * step + part))

    @pl.loop(rounds // DEEP * DEEP, rounds)
    def _(step):
        weigh_two(2 * step)

    for tile in range(tiles):
        top = top_ref[tile]
        peak = jnp.broadcast_to(jnp.max(top, axis=0, keepdims=True), (8, width))
        total = jnp.sum(total_ref[tile] * jnp.exp2(top - peak), axis=0, keepdims=True)
        top_ref[tile] = peak
        share_ref[tile] = 1.0 / jnp.broadcast_to(total, (8, width))
    top_ref[tiles] = jnp.zeros((8, width), jnp.float32)
    share_ref[tiles] = jnp.zeros((8, width), jnp.float32)
    for extra in range(2):
        probs_buf[items + extra] = jnp.zeros((pair, width), jnp.float32)
        top_buf[items + extra] = jnp.zeros((8, width), jnp.float32)

    def value_scores(index, into):
        into[...] = jnp.dot(
            kv_ref[1, area(index), :],
            g_cols[item_tile[index]],
            preferred_element_type=jnp.float32,
        )

    def combine(index, source, low, grad):
        tile = item_tile[index]
        factor = jnp.exp2(top_buf[index] - top_ref[tile]) * share_ref[tile]
        probs = groups(probs_buf[index]) * factor[None]
        low[...] = probs.reshape(pair, width).astype(jnp.bfloat16)
        grad[...] = (
            (probs * (groups(source[...]) - delta_ref[tile][None]) * scale)
            .reshape(pair, width)
            .astype(jnp.bfloat16)
        )

    def add(index, low, grad):
        tile = item_tile[index]
        spot = area(index)
        dkv_acc[1, spot, :] += jnp.dot(
            low[...], g_rows[tile].reshape(width, HD), preferred_element_type=jnp.float32
        )
        dkv_acc[0, spot, :] += jnp.dot(
            grad[...], q_rows[tile].reshape(width, HD), preferred_element_type=jnp.float32
        )
        dq_acc[tile] += lax.dot_general(
            kv_ref[0, spot, :],
            grad[...],
            (((0,), (0,)), ((), ())),
            preferred_element_type=jnp.float32,
        )

    value_scores(0, scores_a)

    def add_two(index):
        value_scores(index + 1, scores_b)
        add(jnp.where(index == 0, items, index - 1), low_b, grad_b)
        combine(index, scores_a, low_a, grad_a)
        value_scores(index + 2, scores_a)
        add(index, low_a, grad_a)
        combine(index + 1, scores_b, low_b, grad_b)

    turns = (items + 2) // 2

    @pl.loop(0, turns // DEEP)
    def _(step):
        for part in range(DEEP):
            add_two(2 * (DEEP * step + part))

    @pl.loop(turns // DEEP * DEEP, turns)
    def _(step):
        add_two(2 * step)

    outs = [pltpu.make_async_copy(dkv_own.at[w], dkv_ref.at[w], sems.at[w]) for w in range(2)]
    for which in range(2):
        @pl.loop(0, count, unroll=4)
        def _(spot):
            place = position_ref[spot]
            dkv_own[which, tile_at(spot), :] = dkv_acc[which, tile_at(place), :].astype(
                jnp.bfloat16
            )

        outs[which].start()

    for tile in range(tiles):
        rows = slice(tile * TILE, (tile + 1) * TILE)
        for h in range(heads):
            lanes = slice(h * HD, (h + 1) * HD)
            dq_own[rows, lanes] = dq_acc[tile, :, lanes].T.astype(jnp.bfloat16)
        copy = pltpu.make_async_copy(dq_own.at[rows], dq_ref.at[rows], sems.at[2 + tile])
        copy.start()
        outs.append(copy)
    for copy in outs:
        copy.wait()


def attention_backward(positions, docs, team, q, g, delta, kv):
    rows, width = q.shape
    heads = width // HD
    tokens = kv.shape[1]
    tiles = rows // TILE
    count = tokens // TILE
    longest = count // 2
    most = sum((longest - i + 1) // 2 for i in range(min(tiles, longest)))
    most = max(most, tiles) + 4
    pair = SPAN * TILE
    smem = pl.BlockSpec(memory_space=pltpu.SMEM)
    hbm = pl.BlockSpec(memory_space=pl.ANY)
    slots = tiles + 1
    stat = pltpu.VMEM((slots, 8, width), jnp.float32)
    return pl.pallas_call(
        functools.partial(attention_kernel, heads, tiles, team),
        out_shape=(
            jax.ShapeDtypeStruct((rows, width), jnp.bfloat16),
            jax.ShapeDtypeStruct((2, tokens, HD), jnp.bfloat16),
        ),
        in_specs=[smem, smem, hbm, hbm, hbm, hbm],
        out_specs=(hbm, hbm),
        scratch_shapes=[
            pltpu.SMEM((count,), jnp.int32),
            pltpu.SMEM((most,), jnp.int32),
            pltpu.SMEM((most,), jnp.int32),
            pltpu.SMEM((most,), jnp.int32),
            pltpu.VMEM((slots, heads, TILE, HD), jnp.bfloat16),
            pltpu.VMEM((slots, heads, TILE, HD), jnp.bfloat16),
            pltpu.VMEM((slots, HD, width), jnp.bfloat16),
            pltpu.VMEM((slots, HD, width), jnp.bfloat16),
            stat,
            pltpu.VMEM((2, tokens + TILE, HD), jnp.bfloat16),
            pltpu.VMEM((pair, TILE), jnp.int32),
            pltpu.VMEM((pair, width), jnp.float32),
            pltpu.VMEM((pair, width), jnp.float32),
            pltpu.VMEM((pair, width), jnp.bfloat16),
            pltpu.VMEM((pair, width), jnp.bfloat16),
            pltpu.VMEM((pair, width), jnp.bfloat16),
            pltpu.VMEM((pair, width), jnp.bfloat16),
            pltpu.VMEM((most, pair, width), jnp.float32),
            pltpu.VMEM((most, 8, width), jnp.float32),
            stat,
            stat,
            stat,
            pltpu.VMEM((slots, HD, width), jnp.float32),
            pltpu.VMEM((2, tokens + TILE, HD), jnp.float32),
            pltpu.VMEM((rows, width), jnp.bfloat16),
            pltpu.VMEM((2, tokens, HD), jnp.bfloat16),
            pltpu.SemaphoreType.DMA((2 + max(2 * heads, tiles),)),
        ],
        compiler_params=pltpu.CompilerParams(vmem_limit_bytes=ATTENTION_LIMIT),
        cost_estimate=pl.CostEstimate(
            flops=rows * width * tokens * 3, bytes_accessed=12 << 20, transcendentals=0
        ),
    )(positions, docs, q.reshape(tiles, TILE, width), g.reshape(tiles, TILE, width), delta, kv)


def bring_kernel(
    team,
    planes,
    q_ref,
    g_ref,
    k_ref,
    v_ref,
    o_ref,
    q_out,
    g_out,
    delta_out,
    kv_out,
    kv_own,
    g_own,
    o_own,
    delta_own,
    load_sem,
    local_sem,
    flat_send,
    flat_recv,
    chain_send,
    chain_recv,
    core_send,
    core_recv,
):
    me = lax.axis_index("ctx")
    slot = me % team
    plane = me // team
    core = slot % 2
    mate = me + 1 - 2 * core
    width = q_out.shape[1]
    span = team * TILE
    tall = pl.ds(pl.multiple_of(slot * TILE, TILE), TILE)
    wide = pl.ds(pl.multiple_of(slot * width, HD), width)

    loads = [
        pltpu.make_async_copy(k_ref, kv_own.at[0], load_sem.at[0]),
        pltpu.make_async_copy(v_ref, kv_own.at[1], load_sem.at[1]),
        pltpu.make_async_copy(g_ref, g_own, load_sem.at[2]),
        pltpu.make_async_copy(o_ref, o_own, load_sem.at[3]),
    ]
    for load in loads:
        load.start()

    barrier = pltpu.get_barrier_semaphore()
    for shift in range(1, team):
        pl.semaphore_signal(
            barrier,
            inc=1,
            device_id=(plane * team + (slot + shift) % team, 0),
            device_id_type=MESH,
        )

    @pl.when(plane < planes - 1)
    def _():
        pl.semaphore_signal(barrier, inc=1, device_id=(me + team, 0), device_id_type=MESH)

    @pl.when(plane > 0)
    def _():
        pl.semaphore_signal(barrier, inc=1, device_id=(me - team, 0), device_id_type=MESH)

    near = jnp.where(plane < planes - 1, 1, 0) + jnp.where(plane > 0, 1, 0)
    pl.semaphore_wait(barrier, team - 1 + near)

    def flat(kind, shift, src, dst):
        return pltpu.make_async_remote_copy(
            src_ref=src,
            dst_ref=dst,
            send_sem=flat_send.at[kind, shift - 1],
            recv_sem=flat_recv.at[kind, slot],
            device_id=(plane * team + (slot + shift) % team, 0),
            device_id_type=MESH,
        )

    loads[0].wait()
    loads[1].wait()
    home = pl.ds(pl.multiple_of(me * TILE, TILE), TILE)
    flats = []
    for shift in range(1, team):
        other = (slot + shift) % team
        lanes = pl.ds(pl.multiple_of(other // 2 * HD, HD), HD)
        copy = flat(
            0, shift, kv_own.at[other % 2, :, lanes], kv_out.at[other % 2, home, :]
        )
        copy.start()
        flats.append(copy)
    locals_ = [
        pltpu.make_async_copy(
            kv_own.at[core, :, pl.ds(pl.multiple_of(slot // 2 * HD, HD), HD)],
            kv_out.at[core, home, :],
            local_sem.at[0],
        ),
        pltpu.make_async_copy(q_ref.at[:, wide], q_out.at[tall, :], local_sem.at[1]),
        pltpu.make_async_copy(g_ref.at[:, wide], g_out.at[tall, :], local_sem.at[2]),
    ]
    for copy in locals_:
        copy.start()
    rest = []
    for kind, (src, dst) in enumerate(((q_ref, q_out), (g_ref, g_out))):
        for shift in range(1, team):
            other = (slot + shift) % team
            lanes = pl.ds(pl.multiple_of(other * width, HD), width)
            copy = flat(1 + kind, shift, src.at[:, lanes], dst.at[tall, :])
            copy.start()
            rest.append(copy)
    locals_[0].wait()
    part_rows = span // SUB
    per_part = team // SUB

    def arrived(kind, source, dst):
        return pltpu.make_async_remote_copy(
            src_ref=dst,
            dst_ref=dst,
            send_sem=flat_send.at[kind, 0],
            recv_sem=flat_recv.at[kind, source],
            device_id=(mate, 0),
            device_id_type=MESH,
        )

    def part(which, sub):
        first = pl.multiple_of(which * span + sub * part_rows, TILE)
        return kv_out.at[core, pl.ds(first, part_rows), :]

    def chain(way, step, which, sub):
        return pltpu.make_async_remote_copy(
            src_ref=part(which, sub),
            dst_ref=part(which, sub),
            send_sem=chain_send.at[way, step, sub],
            recv_sem=chain_recv.at[way, step, sub],
            device_id=(me + team - 2 * way * team, 0),
            device_id_type=MESH,
        )

    def share(index, which, sub):
        return pltpu.make_async_remote_copy(
            src_ref=part(which, sub),
            dst_ref=part(which, sub),
            send_sem=core_send.at[index, sub],
            recv_sem=core_recv.at[index, sub],
            device_id=(mate, 0),
            device_id_type=MESH,
        )

    def up_ok(step):
        return (plane < planes - 1) & (plane - step >= 0)

    def down_ok(step):
        return (plane > 0) & (plane + step <= planes - 1)

    def up_come(step):
        return plane - 1 - step >= 0

    def down_come(step):
        return plane + 1 + step <= planes - 1

    for sub in range(SUB):
        for source in range(sub * per_part, (sub + 1) * per_part):
            @pl.when(slot != source)
            def _():
                arrived(0, source, kv_out.at[core, home, :]).wait_recv()

        @pl.when(up_ok(0))
        def _():
            chain(0, 0, plane, sub).start()

        @pl.when(down_ok(0))
        def _():
            chain(1, 0, plane, sub).start()

        share(0, plane, sub).start()

    loads[2].wait()
    loads[3].wait()
    for index in range(team):
        for head in range(width // HD):
            lanes = slice(index * width + head * HD, index * width + (head + 1) * HD)
            product = g_own[:, lanes].astype(jnp.float32) * o_own[:, lanes].astype(jnp.float32)
            row = jnp.sum(product.T, axis=0, keepdims=True)
            delta_own[index, :, head * HD : (head + 1) * HD] = jnp.broadcast_to(row, (8, HD))
    for shift in range(1, team):
        other = (slot + shift) % team
        copy = flat(3, shift, delta_own.at[other], delta_out.at[slot])
        copy.start()
        rest.append(copy)
    own_delta = pltpu.make_async_copy(delta_own.at[slot], delta_out.at[slot], local_sem.at[3])
    own_delta.start()

    for step in range(planes - 1):
        for sub in range(SUB):
            @pl.when(up_come(step))
            def _():
                chain(0, step, plane - 1 - step, sub).wait_recv()
                if step < planes - 2:
                    @pl.when(up_ok(step + 1))
                    def _():
                        chain(0, step + 1, plane - 1 - step, sub).start()
                share(1 + step, plane - 1 - step, sub).start()

            @pl.when(down_come(step))
            def _():
                chain(1, step, plane + 1 + step, sub).wait_recv()
                if step < planes - 2:
                    @pl.when(down_ok(step + 1))
                    def _():
                        chain(1, step + 1, plane + 1 + step, sub).start()
                share(planes + step, plane + 1 + step, sub).start()

    for sub in range(SUB):
        share(0, plane, sub).wait()
        for step in range(planes - 1):
            @pl.when(up_come(step))
            def _():
                share(1 + step, plane - 1 - step, sub).wait()

            @pl.when(down_come(step))
            def _():
                share(planes + step, plane + 1 + step, sub).wait()

            @pl.when(up_ok(step))
            def _():
                chain(0, step, plane - step, sub).wait_send()

            @pl.when(down_ok(step))
            def _():
                chain(1, step, plane + step, sub).wait_send()

    for copy in locals_[1:] + [own_delta]:
        copy.wait()
    for copy in rest + flats:
        copy.wait_send()
    for source in range(team):
        @pl.when(slot != source)
        def _():
            arrived(1, source, q_out.at[tall, :]).wait_recv()
            arrived(2, source, g_out.at[tall, :]).wait_recv()
            arrived(3, source, delta_out.at[slot]).wait_recv()


def bring(team, planes, queries, out_grad, key_states, value_states, outputs):
    rows, columns = queries.shape
    width = columns // team
    tokens = rows * team * planes
    vmem = pl.BlockSpec(memory_space=pltpu.VMEM)
    hbm = pl.BlockSpec(memory_space=pltpu.HBM)
    dma = pltpu.SemaphoreType.DMA
    return pl.pallas_call(
        functools.partial(bring_kernel, team, planes),
        out_shape=(
            jax.ShapeDtypeStruct((rows * team, width), jnp.bfloat16),
            jax.ShapeDtypeStruct((rows * team, width), jnp.bfloat16),
            jax.ShapeDtypeStruct((team, 8, width), jnp.float32),
            jax.ShapeDtypeStruct((2, tokens, HD), jnp.bfloat16),
        ),
        in_specs=[hbm, hbm, hbm, hbm, hbm],
        out_specs=(hbm, hbm, hbm, hbm),
        scratch_shapes=[
            pltpu.VMEM((2, rows, key_states.shape[1]), jnp.bfloat16),
            pltpu.VMEM((rows, columns), jnp.bfloat16),
            pltpu.VMEM((rows, columns), jnp.bfloat16),
            pltpu.VMEM((team, 8, width), jnp.float32),
            dma((4,)),
            dma((4,)),
            dma((4, team - 1)),
            dma((4, team)),
            dma((2, planes - 1, SUB)),
            dma((2, planes - 1, SUB)),
            dma((2 * planes - 1, SUB)),
            dma((2 * planes - 1, SUB)),
        ],
        compiler_params=pltpu.CompilerParams(
            collective_id=0, has_side_effects=True, vmem_limit_bytes=60 * 1024 * 1024
        ),
        cost_estimate=pl.CostEstimate(flops=0, bytes_accessed=60 << 20, transcendentals=0),
    )(queries, out_grad, key_states, value_states, outputs)


def return_kernel(
    team,
    planes,
    dq_ref,
    dkv_ref,
    dq_out,
    dkv_out,
    own,
    mate_in,
    chain_in,
    chain_own,
    total,
    local_sem,
    dq_send,
    dq_recv,
    flat_send,
    flat_recv,
    chain_send,
    chain_recv,
    core_send,
    core_recv,
):
    me = lax.axis_index("ctx")
    slot = me % team
    plane = me // team
    core = slot % 2
    mate = me + 1 - 2 * core
    width = dq_ref.shape[1]
    span = team * TILE
    part_rows = span // FINE
    per_part = team // FINE

    load = pltpu.make_async_copy(dkv_ref.at[core], own, local_sem.at[2])
    load.start()
    barrier = pltpu.get_barrier_semaphore()
    for shift in range(1, team):
        pl.semaphore_signal(
            barrier,
            inc=1,
            device_id=(plane * team + (slot + shift) % team, 0),
            device_id_type=MESH,
        )

    @pl.when(plane < planes - 1)
    def _():
        pl.semaphore_signal(barrier, inc=1, device_id=(me + team, 0), device_id_type=MESH)

    @pl.when(plane > 0)
    def _():
        pl.semaphore_signal(barrier, inc=1, device_id=(me - team, 0), device_id_type=MESH)

    near = jnp.where(plane < planes - 1, 1, 0) + jnp.where(plane > 0, 1, 0)
    pl.semaphore_wait(barrier, team - 1 + near)

    def rows_of(which, sub):
        return pl.ds(pl.multiple_of(which * span + sub * part_rows, TILE), part_rows)

    def inner(sub):
        return pl.ds(sub * part_rows, part_rows)

    def tile_rows(which):
        return pl.ds(pl.multiple_of(which * TILE, TILE), TILE)

    half = plane // (planes // 2)
    depth = plane * (1 - half) + (planes - 1 - plane) * half
    ahead = me + team * (1 - 2 * half)
    behind = me - team * (1 - 2 * half)

    def target_plane(index):
        return (planes - 1 - index) * (1 - half) + index * half

    shares = {}
    for index in range(planes):
        for sub in range(FINE):
            copy = pltpu.make_async_remote_copy(
                src_ref=dkv_ref.at[1 - core, rows_of(target_plane(index), sub), :],
                dst_ref=mate_in.at[index, inner(sub)],
                send_sem=core_send.at[index, sub],
                recv_sem=core_recv.at[index, sub],
                device_id=(mate, 0),
                device_id_type=MESH,
            )
            copy.start()
            shares[index, sub] = copy

    wide = pl.ds(pl.multiple_of(slot * width, HD), width)
    rest = []
    own_dq = pltpu.make_async_copy(
        dq_ref.at[tile_rows(slot), :], dq_out.at[:, wide], local_sem.at[0]
    )
    own_dq.start()
    for shift in range(1, team):
        other = (slot + shift) % team
        copy = pltpu.make_async_remote_copy(
            src_ref=dq_ref.at[tile_rows(other), :],
            dst_ref=dq_out.at[:, wide],
            send_sem=dq_send.at[shift - 1],
            recv_sem=dq_recv.at[shift - 1],
            device_id=(plane * team + other, 0),
            device_id_type=MESH,
        )
        copy.start()
        rest.append(copy)

    def chain(source, into, index, sub, device):
        return pltpu.make_async_remote_copy(
            src_ref=chain_own.at[source, index, inner(sub)],
            dst_ref=chain_in.at[into, index, inner(sub)],
            send_sem=chain_send.at[source, index, sub],
            recv_sem=chain_recv.at[into, index, sub],
            device_id=(device, 0),
            device_id_type=MESH,
        )

    def local_sum(index, sub):
        shares[index, sub].wait_recv()
        return own[rows_of(target_plane(index), sub), :].astype(jnp.float32) + mate_in[
            index, inner(sub)
        ].astype(jnp.float32)

    def come(way, index, sub):
        chain(0, way, index, sub, mate).wait_recv()
        return chain_in[way, index, inner(sub)].astype(jnp.float32)

    load.wait()
    lanes = pl.ds(pl.multiple_of(slot // 2 * HD, HD), HD)
    def flat(target):
        return pltpu.make_async_remote_copy(
            src_ref=total.at[tile_rows(target), :],
            dst_ref=dkv_out.at[core, :, lanes],
            send_sem=flat_send.at[target],
            recv_sem=flat_recv.at[slot],
            device_id=(plane * team + target, 0),
            device_id_type=MESH,
        )

    def finish(value, sub):
        total[inner(sub)] = value.astype(jnp.bfloat16)
        for target in range(sub * per_part, (sub + 1) * per_part):
            @pl.when(slot != target)
            def _():
                flat(target).start()

    pieces = [(index, sub) for index in range(planes - 1) for sub in range(FINE)]

    @pl.when(depth == 0)
    def _():
        moves = []
        for index, sub in pieces:
            chain_own[0, index, inner(sub)] = local_sum(index, sub).astype(jnp.bfloat16)
            if len(moves) >= FLIGHT:
                moves[-FLIGHT].wait_send()
            move = chain(0, 0, index, sub, ahead)
            move.start()
            moves.append(move)
        for sub in range(FINE):
            finish(local_sum(planes - 1, sub) + come(1, 0, sub), sub)
        for move in moves[-FLIGHT:]:
            move.wait_send()

    @pl.when(depth == 1)
    def _():
        moves = []
        near = [(0, 0, index, sub) for index in range(2) for sub in range(FINE)]
        far = [(1, 1, 0, sub) for sub in range(FINE)]
        line = near[:FINE]
        for step in range(FINE):
            line.extend((far[step], near[FINE + step]))
        for way, source, index, sub in line:
            share = planes - 1 if way else index
            chain_own[source, index, inner(sub)] = (
                local_sum(share, sub) + come(way, index, sub)
            ).astype(jnp.bfloat16)
            move = chain(source, 1, index, sub, behind if way else ahead)
            move.start()
            moves.append(move)
        for sub in range(FINE):
            finish(local_sum(2, sub) + come(1, 1, sub) + come(0, 2, sub), sub)
        for move in moves:
            move.wait_send()

    own_dkv = pltpu.make_async_copy(
        total.at[tile_rows(slot), :], dkv_out.at[core, :, lanes], local_sem.at[1]
    )
    own_dkv.start()
    own_dq.wait()
    own_dkv.wait()
    for copy in shares.values():
        copy.wait_send()
    for copy in rest:
        copy.wait()
    for target in range(team):
        @pl.when(slot != target)
        def _():
            flat(target).wait_send()
            pltpu.make_async_remote_copy(
                src_ref=total.at[tile_rows(slot), :],
                dst_ref=dkv_out.at[core, :, lanes],
                send_sem=flat_send.at[target],
                recv_sem=flat_recv.at[target],
                device_id=(mate, 0),
                device_id_type=MESH,
            ).wait_recv()


def give_back(team, planes, dq, dkv):
    tall, width = dq.shape
    rows = tall // team
    heads = team // 2
    hbm = pl.BlockSpec(memory_space=pl.ANY)
    dma = pltpu.SemaphoreType.DMA
    part = pltpu.VMEM((2, planes - 1, tall, HD), jnp.bfloat16)
    return pl.pallas_call(
        functools.partial(return_kernel, team, planes),
        out_shape=(
            jax.ShapeDtypeStruct((rows, width * team), jnp.bfloat16),
            jax.ShapeDtypeStruct((2, rows, heads * HD), jnp.bfloat16),
        ),
        in_specs=[hbm, hbm],
        out_specs=(hbm, hbm),
        scratch_shapes=[
            pltpu.VMEM((planes * tall, HD), jnp.bfloat16),
            pltpu.VMEM((planes, tall, HD), jnp.bfloat16),
            part,
            part,
            pltpu.VMEM((tall, HD), jnp.bfloat16),
            dma((3,)),
            dma((team - 1,)),
            dma((team - 1,)),
            dma((team,)),
            dma((team,)),
            dma((2, planes - 1, FINE)),
            dma((2, planes - 1, FINE)),
            dma((planes, FINE)),
            dma((planes, FINE)),
        ],
        compiler_params=pltpu.CompilerParams(
            collective_id=1, has_side_effects=True, vmem_limit_bytes=GIVE_LIMIT
        ),
        cost_estimate=pl.CostEstimate(flops=0, bytes_accessed=60 << 20, transcendentals=0),
    )(dq, dkv)


def local_planes(queries, key_states, value_states, outputs, out_grad, doc_of_tile, tile_position):
    team = 2 * (key_states.shape[1] // HD)
    planes = lax.axis_size("ctx") // team
    q, g, delta, kv = bring(team, planes, queries, out_grad, key_states, value_states, outputs)
    dq, dkv = attention_backward(tile_position, doc_of_tile, team, q, g, delta, kv)
    dq, dkv = give_back(team, planes, dq, dkv)
    return dq, dkv[0], dkv[1]


def local_any(queries, key_states, value_states, outputs, out_grad, doc_of_tile, tile_position):
    rows = queries.shape[0]
    kv_heads = key_states.shape[1] // HD
    head_count = lax.axis_size("head")
    ctx_count = lax.axis_size("ctx")
    ctx_index = lax.axis_index("ctx")
    split = kv_heads * head_count
    team = kv_heads
    parts = ctx_count // team
    near = [[b * team + s for s in range(team)] for b in range(parts)]
    far = [[b * team + s for b in range(parts)] for s in range(team)]

    def swap(value, split_axis, concat_axis):
        if head_count > 1:
            return lax.all_to_all(value, "head", split_axis, concat_axis, tiled=True)
        return lax.all_to_all(
            value, "ctx", split_axis, concat_axis, axis_index_groups=near, tiled=True
        )

    heads = queries.shape[1] // split // HD
    products = out_grad.astype(jnp.float32) * outputs.astype(jnp.float32)
    delta = jnp.sum(products.reshape(rows, split * heads, HD), axis=-1)
    kv = jnp.concatenate([key_states, value_states], axis=1)
    if head_count == 1:
        kv = kv.reshape(rows, 2, team, HD).transpose(0, 2, 1, 3).reshape(rows, team * 2 * HD)
        kv = swap(kv, 1, 0)
    kv = lax.all_gather(kv, "ctx", axis=0, tiled=True, axis_index_groups=far)
    kv = kv.reshape(-1, 2, HD).transpose(1, 0, 2)
    qd = jnp.concatenate(
        [
            queries.reshape(rows, split, heads * HD),
            out_grad.reshape(rows, split, heads * HD),
        ],
        axis=2,
    ).reshape(rows, split * 2 * heads * HD)
    qd = swap(qd, 1, 0)
    delta = swap(delta, 1, 0)
    tiles = qd.shape[0] // TILE
    delta = jnp.transpose(delta.reshape(tiles, TILE, heads), (0, 2, 1)).reshape(
        tiles, 1, heads * TILE
    )
    delta = jnp.broadcast_to(delta, (tiles, 8, heads * TILE))
    width = heads * HD
    dq, dkv = attention_backward(
        tile_position, doc_of_tile, team, qd[:, :width], qd[:, width:], delta, kv
    )
    if head_count == 1:
        dq = swap(dq, 0, 1)
    dkv = dkv.transpose(1, 0, 2).reshape(-1, 2 * HD)
    dkv = lax.all_to_all(dkv, "ctx", 0, 0, axis_index_groups=far, tiled=True)
    dkv = jnp.sum(dkv.reshape(parts, -1, 2 * HD).astype(jnp.float32), axis=0).astype(jnp.bfloat16)
    if head_count == 1:
        dkv = swap(dkv, 0, 1)
    dkv = dkv.reshape(dkv.shape[0], kv_heads, 2, HD)
    return (
        dq,
        dkv[:, :, 0].reshape(-1, kv_heads * HD),
        dkv[:, :, 1].reshape(-1, kv_heads * HD),
    )


def solution(mesh):
    placed = (
        P(("ctx", "head"), None),
        P("ctx", "head"),
        P("ctx", "head"),
        P(("ctx", "head"), None),
        P(("ctx", "head"), None),
        P(),
        P(),
    )
    slabs = mesh.shape["head"] == 1 and mesh.shape["ctx"] == 32
    return jax.shard_map(
        local_planes if slabs else local_any,
        mesh=mesh,
        in_specs=placed,
        out_specs=(P("ctx", "head"), P("ctx", "head"), P("ctx", "head")),
        check_vma=False,
    )
```

profile of v0, /device:TPU:15, one launch (start us, length us, event | category | flops | bytes accessed | tf_op | source)
XLA Modules:
  0.0 83.3 jit_solution(13616504591355694716)
XLA Ops:
  0.6 32.0 %shard_map.94 = (bf16[1024,512]{1,0:T(8,128)(2,1)}, bf16[1024,512]{1,0:T(8,128)(2,1)}, f32[8,8,512]{2,1,0:T(8,128)}, bf16[2,4096,128]{2,1,0:T(8,128)(2,1)}) custom-call(bf16[128,4096]{1,0:T(8,128)(2,1)} %q_ref.1, bf16[128,4096]{1,0:T(8,128)(2,1)} %g_ref.1, bf16[128,512]{1,0:T(8,128)(2,1)} %k_ref.1, bf16[128,512]{1,0:T(8,128)(2,1)} %v_ref.1, ...), custom_call_target="tpu_custom_call" | custom-call | bytes 62914560 | tf_op jit(solution)/shard_map/pallas_call | solution.py:592
  32.6 22.6 %shard_map.95 = (bf16[1024,512]{1,0:T(8,128)(2,1)}, bf16[2,4096,128]{2,1,0:T(8,128)(2,1)}) custom-call(s32[32]{0:T(128)} %position_ref.1, s32[32]{0:T(128)} %doc_ref.1, bf16[8,128,512]{2,1,0:T(8,128)(2,1)} %bitcast.6, bf16[8,128,512]{2,1,0:T(8,128)(2,1)} %bitcast.7, f32[8,8,512]{2,1,0:T(8,128)} %get-tuple-element.13.delta_hbm, ...), custom_call_target="tpu_custom_call" | custom-call | flops 6442450944 | bytes 12582912 | tf_op jit(solution)/shard_map/pallas_call | solution.py:303
  55.2 26.4 %shard_map.96 = (bf16[128,4096]{1,0:T(8,128)(2,1)S(1)}, bf16[2,128,512]{2,1,0:T(8,128)(2,1)S(1)}) custom-call(bf16[1024,512]{1,0:T(8,128)(2,1)} %get-tuple-element.15.dq_ref, bf16[2,4096,128]{2,1,0:T(8,128)(2,1)} %get-tuple-element.16.dkv_ref), custom_call_target="tpu_custom_call" | custom-call | bytes 62914560 | tf_op jit(solution)/shard_map/pallas_call | solution.py:835
  81.6 0.7 slice_bitcast_fusion
  82.4 1.0 %copy.11 = bf16[128,4096]{1,0:T(8,128)(2,1)} copy(bf16[128,4096]{1,0:T(8,128)(2,1)S(1)} %get-tuple-element.24) | data formatting | bytes 2097152
where the time goes:
time: 83.8 us; the launch traced here: 83.3 us
  Pallas kernels  81 us (97%)
  local copies, waits for them, and re-layouts  1.69 us (2%)
    pallas_call x1, Pallas kernels, bring(): pl.pallas_call(functools.partial(bring_kernel, team, planes), out_shape=(...  32 us
    pallas_call x1, Pallas kernels, give_back(): pl.pallas_call(functools.partial(return_kernel, team, planes), out_shape=...  26.4 us
    pallas_call x1, Pallas kernels, attention_backward(): pl.pallas_call(functools.partial(attention_kernel, heads, tiles, team), o...  22.6 us

commit v1 on v0

--- a/solution.py
+++ b/solution.py
@@ -108,16 +108,16 @@
     def listed(tile, total):
         place = position_ref[block * tiles + tile]
         start = start_ref[place]
-        pieces = (place - start + 2) // 2
-
-        @pl.loop(0, pieces)
+        full = (place - start) // 2
+        put(tile, tile, start + 2 * full, (place - start - 2 * full) * TILE)
+
+        @pl.loop(0, full)
         def _(step):
-            first = start + 2 * step
-            put(total + step, tile, first, (place - first) * TILE)
-
-        return total + pieces
-
-    items = lax.fori_loop(0, tiles, listed, jnp.int32(0))
+            put(total + step, tile, start + 2 * step, pair)
+
+        return total + full
+
+    items = lax.fori_loop(0, tiles, listed, jnp.int32(tiles))
     for extra in range(4):
         put(items + extra, tiles, 0, pair)
 
@@ -132,7 +132,7 @@
     g_cols[tiles] = jnp.zeros((HD, width), jnp.bfloat16)
     q_rows[tiles] = jnp.zeros((heads, TILE, HD), jnp.bfloat16)
     g_rows[tiles] = jnp.zeros((heads, TILE, HD), jnp.bfloat16)
-    delta_ref[tiles] = jnp.zeros((8, width), jnp.float32)
+    delta_ref[tiles] = jnp.zeros((1, width), jnp.float32)
     kv_ref[:, count * TILE :, :] = jnp.zeros((2, TILE, HD), jnp.bfloat16)
     low_b[...] = jnp.zeros_like(low_b)
     grad_b[...] = jnp.zeros_like(grad_b)
@@ -163,12 +163,13 @@
             preferred_element_type=jnp.float32,
         )
 
-    def weigh(index, source):
+    def weigh(index, source, edge):
         tile = item_tile[index]
-        gap = jnp.concatenate([gap_ref[...]] * heads, axis=1)
-        scores = groups(
-            jnp.where(gap <= item_bound[index], source[...] * (scale * LOG2E), LOW)
-        )
+        scores = source[...] * (scale * LOG2E)
+        if edge:
+            gap = jnp.concatenate([gap_ref[...]] * heads, axis=1)
+            scores = jnp.where(gap <= item_bound[index], scores, LOW)
+        scores = groups(scores)
         old = top_ref[tile]
         top = jnp.maximum(old, jnp.max(scores, axis=0))
         probs = jnp.exp2(scores - top[None])
@@ -179,20 +180,24 @@
 
     score(0, scores_a)
 
-    def weigh_two(index):
+    def weigh_two(index, edge=False):
         score(index + 1, scores_b)
-        weigh(index, scores_a)
+        weigh(index, scores_a, edge)
         score(index + 2, scores_a)
-        weigh(index + 1, scores_b)
-
+        weigh(index + 1, scores_b, edge)
+
+    edges = (tiles + 1) // 2
     rounds = (items + 1) // 2
-
-    @pl.loop(0, rounds // DEEP)
+    for part in range(edges):
+        weigh_two(2 * part, edge=True)
+    deep = edges + (rounds - edges) // DEEP * DEEP
+
+    @pl.loop(0, (rounds - edges) // DEEP)
     def _(step):
         for part in range(DEEP):
-            weigh_two(2 * (DEEP * step + part))
-
-    @pl.loop(rounds // DEEP * DEEP, rounds)
+            weigh_two(2 * (edges + DEEP * step + part))
+
+    @pl.loop(deep, rounds)
     def _(step):
         weigh_two(2 * step)
 
@@ -317,7 +322,7 @@
             pltpu.VMEM((slots, heads, TILE, HD), jnp.bfloat16),
             pltpu.VMEM((slots, HD, width), jnp.bfloat16),
             pltpu.VMEM((slots, HD, width), jnp.bfloat16),
-            stat,
+            pltpu.VMEM((slots, 1, width), jnp.float32),
             pltpu.VMEM((2, tokens + TILE, HD), jnp.bfloat16),
             pltpu.VMEM((pair, TILE), jnp.int32),
             pltpu.VMEM((pair, width), jnp.float32),
@@ -522,7 +527,7 @@
             lanes = slice(index * width + head * HD, index * width + (head + 1) * HD)
             product = g_own[:, lanes].astype(jnp.float32) * o_own[:, lanes].astype(jnp.float32)
             row = jnp.sum(product.T, axis=0, keepdims=True)
-            delta_own[index, :, head * HD : (head + 1) * HD] = jnp.broadcast_to(row, (8, HD))
+            delta_own[index, :, head * HD : (head + 1) * HD] = row
     for shift in range(1, team):
         other = (slot + shift) % team
         copy = flat(3, shift, delta_own.at[other], delta_out.at[slot])
@@ -594,7 +599,7 @@
         out_shape=(
             jax.ShapeDtypeStruct((rows * team, width), jnp.bfloat16),
             jax.ShapeDtypeStruct((rows * team, width), jnp.bfloat16),
-            jax.ShapeDtypeStruct((team, 8, width), jnp.float32),
+            jax.ShapeDtypeStruct((team, 1, width), jnp.float32),
             jax.ShapeDtypeStruct((2, tokens, HD), jnp.bfloat16),
         ),
         in_specs=[hbm, hbm, hbm, hbm, hbm],
@@ -603,7 +608,7 @@
             pltpu.VMEM((2, rows, key_states.shape[1]), jnp.bfloat16),
             pltpu.VMEM((rows, columns), jnp.bfloat16),
             pltpu.VMEM((rows, columns), jnp.bfloat16),
-            pltpu.VMEM((team, 8, width), jnp.float32),
+            pltpu.VMEM((team, 1, width), jnp.float32),
             dma((4,)),
             dma((4,)),
             dma((4, team - 1)),
@@ -702,8 +707,9 @@
                 device_id=(mate, 0),
                 device_id_type=MESH,
             )
-            copy.start()
             shares[index, sub] = copy
+    for sub in range(FINE):
+        shares[0, sub].start()
 
     wide = pl.ds(pl.multiple_of(slot * width, HD), width)
     rest = []
@@ -745,6 +751,11 @@
         return chain_in[way, index, inner(sub)].astype(jnp.float32)
 
     load.wait()
+    for sub in range(FINE):
+        shares[0, sub].wait_send()
+    for index in (planes - 1, *range(1, planes - 1)):
+        for sub in range(FINE):
+            shares[index, sub].start()
     lanes = pl.ds(pl.multiple_of(slot // 2 * HD, HD), HD)
     def flat(target):
         return pltpu.make_async_remote_copy(
@@ -807,8 +818,9 @@
     own_dkv.start()
     own_dq.wait()
     own_dkv.wait()
-    for copy in shares.values():
-        copy.wait_send()
+    for index in range(1, planes):
+        for sub in range(FINE):
+            shares[index, sub].wait_send()
     for copy in rest:
         copy.wait()
     for target in range(team):
@@ -913,7 +925,6 @@
     delta = jnp.transpose(delta.reshape(tiles, TILE, heads), (0, 2, 1)).reshape(
         tiles, 1, heads * TILE
     )
-    delta = jnp.broadcast_to(delta, (tiles, 8, heads * TILE))
     width = heads * HD
     dq, dkv = attention_backward(
         tile_position, doc_of_tile, team, qd[:, :width], qd[:, width:], delta, kv

time: 83.8 us -> 80.5 us (0.961)
  Pallas kernels: 81 us -> 77.3 us
    pallas_call x1, Pallas kernels: 22.6 us -> 15.7 us  [attention_backward(): pl.pallas_call(functools.partial(attention_kernel, heads, tiles, team), o...]
    pallas_call x1, Pallas kernels: 26.4 us -> 30.7 us  [give_back(): pl.pallas_call(functools.partial(return_kernel, team, planes), out_shape=...]
    pallas_call x1, Pallas kernels: 32 us -> 30.9 us  [bring(): pl.pallas_call(functools.partial(bring_kernel, team, planes), out_shape=(...]
where the time goes in v1:
time: 80.5 us; the launch traced here: 79.7 us
  Pallas kernels  77.3 us (96%)
  local copies, waits for them, and re-layouts  1.69 us (2%)
    pallas_call x1, Pallas kernels, bring(): pl.pallas_call(functools.partial(bring_kernel, team, planes), out_shape=(...  30.9 us
    pallas_call x1, Pallas kernels, give_back(): pl.pallas_call(functools.partial(return_kernel, team, planes), out_shape=...  30.7 us
    pallas_call x1, Pallas kernels, attention_backward(): pl.pallas_call(functools.partial(attention_kernel, heads, tiles, team), o...  15.7 us

profile of v1, /device:TPU:15, one launch (start us, length us, event | category | flops | bytes accessed | tf_op | source)
XLA Modules:
  0.0 79.7 jit_solution(17511135216162501471)
XLA Ops:
  0.6 30.9 %shard_map.94 = (bf16[1024,512]{1,0:T(8,128)(2,1)}, bf16[1024,512]{1,0:T(8,128)(2,1)}, f32[8,1,512]{2,1,0:T(1,128)}, bf16[2,4096,128]{2,1,0:T(8,128)(2,1)}) custom-call(bf16[128,4096]{1,0:T(8,128)(2,1)} %q_ref.1, bf16[128,4096]{1,0:T(8,128)(2,1)} %g_ref.1, bf16[128,512]{1,0:T(8,128)(2,1)} %k_ref.1, bf16[128,512]{1,0:T(8,128)(2,1)} %v_ref.1, ...), custom_call_target="tpu_custom_call" | custom-call | bytes 62914560 | tf_op jit(solution)/shard_map/pallas_call | solution.py:597
  31.6 15.7 %shard_map.95 = (bf16[1024,512]{1,0:T(8,128)(2,1)}, bf16[2,4096,128]{2,1,0:T(8,128)(2,1)}) custom-call(s32[32]{0:T(128)} %position_ref.1, s32[32]{0:T(128)} %doc_ref.1, bf16[8,128,512]{2,1,0:T(8,128)(2,1)} %bitcast.6, bf16[8,128,512]{2,1,0:T(8,128)(2,1)} %bitcast.7, f32[8,1,512]{2,1,0:T(1,128)} %get-tuple-element.13.delta_hbm, ...), custom_call_target="tpu_custom_call" | custom-call | flops 6442450944 | bytes 12582912 | tf_op jit(solution)/shard_map/pallas_call | solution.py:308
  47.3 30.7 %shard_map.96 = (bf16[128,4096]{1,0:T(8,128)(2,1)S(1)}, bf16[2,128,512]{2,1,0:T(8,128)(2,1)S(1)}) custom-call(bf16[1024,512]{1,0:T(8,128)(2,1)} %get-tuple-element.15.dq_ref, bf16[2,4096,128]{2,1,0:T(8,128)(2,1)} %get-tuple-element.16.dkv_ref), custom_call_target="tpu_custom_call" | custom-call | bytes 62914560 | tf_op jit(solution)/shard_map/pallas_call | solution.py:847
  78.0 0.7 slice_bitcast_fusion
  78.7 1.0 %copy.11 = bf16[128,4096]{1,0:T(8,128)(2,1)} copy(bf16[128,4096]{1,0:T(8,128)(2,1)S(1)} %get-tuple-element.24) | data formatting | bytes 2097152

commit v2 on v1

--- a/solution.py
+++ b/solution.py
@@ -14,7 +14,7 @@
 LOG2E = 1.4426950408889634
 DEEP = 4
 SUB = 2
-FINE = 4
+FINE = 2
 FLIGHT = 2
 GIVE_LIMIT = 52 * 1024 * 1024
 ATTENTION_LIMIT = 56 * 1024 * 1024
@@ -140,7 +140,7 @@
     for copy in heads_in:
         copy.wait()
 
-    @pl.loop(0, tiles)
+    @pl.loop(0, tiles, unroll=tiles)
     def _(tile):
         for h in range(heads):
             lanes = slice(h * HD, (h + 1) * HD)
@@ -653,9 +653,7 @@
     core = slot % 2
     mate = me + 1 - 2 * core
     width = dq_ref.shape[1]
-    span = team * TILE
-    part_rows = span // FINE
-    per_part = team // FINE
+    part_rows = TILE // FINE
 
     load = pltpu.make_async_copy(dkv_ref.at[core], own, local_sem.at[2])
     load.start()
@@ -679,9 +677,6 @@
     near = jnp.where(plane < planes - 1, 1, 0) + jnp.where(plane > 0, 1, 0)
     pl.semaphore_wait(barrier, team - 1 + near)
 
-    def rows_of(which, sub):
-        return pl.ds(pl.multiple_of(which * span + sub * part_rows, TILE), part_rows)
-
     def inner(sub):
         return pl.ds(sub * part_rows, part_rows)
 
@@ -700,8 +695,8 @@
     for index in range(planes):
         for sub in range(FINE):
             copy = pltpu.make_async_remote_copy(
-                src_ref=dkv_ref.at[1 - core, rows_of(target_plane(index), sub), :],
-                dst_ref=mate_in.at[index, inner(sub)],
+                src_ref=dkv_ref.at[1 - core, target_plane(index), :, inner(sub), :],
+                dst_ref=mate_in.at[index, :, inner(sub), :],
                 send_sem=core_send.at[index, sub],
                 recv_sem=core_recv.at[index, sub],
                 device_id=(mate, 0),
@@ -732,8 +727,8 @@
 
     def chain(source, into, index, sub, device):
         return pltpu.make_async_remote_copy(
-            src_ref=chain_own.at[source, index, inner(sub)],
-            dst_ref=chain_in.at[into, index, inner(sub)],
+            src_ref=chain_own.at[source, index, :, inner(sub), :],
+            dst_ref=chain_in.at[into, index, :, inner(sub), :],
             send_sem=chain_send.at[source, index, sub],
             recv_sem=chain_recv.at[into, index, sub],
             device_id=(device, 0),
@@ -742,13 +737,13 @@
 
     def local_sum(index, sub):
         shares[index, sub].wait_recv()
-        return own[rows_of(target_plane(index), sub), :].astype(jnp.float32) + mate_in[
-            index, inner(sub)
+        return own[target_plane(index), :, inner(sub), :].astype(jnp.float32) + mate_in[
+            index, :, inner(sub), :
         ].astype(jnp.float32)
 
     def come(way, index, sub):
         chain(0, way, index, sub, mate).wait_recv()
-        return chain_in[way, index, inner(sub)].astype(jnp.float32)
+        return chain_in[way, index, :, inner(sub), :].astype(jnp.float32)
 
     load.wait()
     for sub in range(FINE):
@@ -757,22 +752,21 @@
         for sub in range(FINE):
             shares[index, sub].start()
     lanes = pl.ds(pl.multiple_of(slot // 2 * HD, HD), HD)
-    def flat(target):
+    def flat(shift, sub):
+        target = (slot + shift) % team
         return pltpu.make_async_remote_copy(
-            src_ref=total.at[tile_rows(target), :],
-            dst_ref=dkv_out.at[core, :, lanes],
-            send_sem=flat_send.at[target],
-            recv_sem=flat_recv.at[slot],
+            src_ref=total.at[target, inner(sub), :],
+            dst_ref=dkv_out.at[core, inner(sub), lanes],
+            send_sem=flat_send.at[shift - 1, sub],
+            recv_sem=flat_recv.at[shift - 1, sub],
             device_id=(plane * team + target, 0),
             device_id_type=MESH,
         )
 
     def finish(value, sub):
-        total[inner(sub)] = value.astype(jnp.bfloat16)
-        for target in range(sub * per_part, (sub + 1) * per_part):
-            @pl.when(slot != target)
-            def _():
-                flat(target).start()
+        total[:, inner(sub), :] = value.astype(jnp.bfloat16)
+        for shift in range(1, team):
+            flat(shift, sub).start()
 
     pieces = [(index, sub) for index in range(planes - 1) for sub in range(FINE)]
 
@@ -780,7 +774,7 @@
     def _():
         moves = []
         for index, sub in pieces:
-            chain_own[0, index, inner(sub)] = local_sum(index, sub).astype(jnp.bfloat16)
+            chain_own[0, index, :, inner(sub), :] = local_sum(index, sub).astype(jnp.bfloat16)
             if len(moves) >= FLIGHT:
                 moves[-FLIGHT].wait_send()
             move = chain(0, 0, index, sub, ahead)
@@ -801,7 +795,7 @@
             line.extend((far[step], near[FINE + step]))
         for way, source, index, sub in line:
             share = planes - 1 if way else index
-            chain_own[source, index, inner(sub)] = (
+            chain_own[source, index, :, inner(sub), :] = (
                 local_sum(share, sub) + come(way, index, sub)
             ).astype(jnp.bfloat16)
             move = chain(source, 1, index, sub, behind if way else ahead)
@@ -813,7 +807,7 @@
             move.wait_send()
 
     own_dkv = pltpu.make_async_copy(
-        total.at[tile_rows(slot), :], dkv_out.at[core, :, lanes], local_sem.at[1]
+        total.at[slot], dkv_out.at[core, :, lanes], local_sem.at[1]
     )
     own_dkv.start()
     own_dq.wait()
@@ -823,18 +817,9 @@
             shares[index, sub].wait_send()
     for copy in rest:
         copy.wait()
-    for target in range(team):
-        @pl.when(slot != target)
-        def _():
-            flat(target).wait_send()
-            pltpu.make_async_remote_copy(
-                src_ref=total.at[tile_rows(slot), :],
-                dst_ref=dkv_out.at[core, :, lanes],
-                send_sem=flat_send.at[target],
-                recv_sem=flat_recv.at[target],
-                device_id=(mate, 0),
-                device_id_type=MESH,
-            ).wait_recv()
+    for sub in range(FINE):
+        for shift in range(1, team):
+            flat(shift, sub).wait()
 
 
 def give_back(team, planes, dq, dkv):
@@ -843,7 +828,7 @@
     heads = team // 2
     hbm = pl.BlockSpec(memory_space=pl.ANY)
     dma = pltpu.SemaphoreType.DMA
-    part = pltpu.VMEM((2, planes - 1, tall, HD), jnp.bfloat16)
+    part = pltpu.VMEM((2, planes - 1, team, rows, HD), jnp.bfloat16)
     return pl.pallas_call(
         functools.partial(return_kernel, team, planes),
         out_shape=(
@@ -853,16 +838,16 @@
         in_specs=[hbm, hbm],
         out_specs=(hbm, hbm),
         scratch_shapes=[
-            pltpu.VMEM((planes * tall, HD), jnp.bfloat16),
-            pltpu.VMEM((planes, tall, HD), jnp.bfloat16),
+            pltpu.VMEM((planes, team, rows, HD), jnp.bfloat16),
+            pltpu.VMEM((planes, team, rows, HD), jnp.bfloat16),
             part,
             part,
-            pltpu.VMEM((tall, HD), jnp.bfloat16),
+            pltpu.VMEM((team, rows, HD), jnp.bfloat16),
             dma((3,)),
             dma((team - 1,)),
             dma((team - 1,)),
-            dma((team,)),
-            dma((team,)),
+            dma((team - 1, FINE)),
+            dma((team - 1, FINE)),
             dma((2, planes - 1, FINE)),
             dma((2, planes - 1, FINE)),
             dma((planes, FINE)),
@@ -872,7 +857,7 @@
             collective_id=1, has_side_effects=True, vmem_limit_bytes=GIVE_LIMIT
         ),
         cost_estimate=pl.CostEstimate(flops=0, bytes_accessed=60 << 20, transcendentals=0),
-    )(dq, dkv)
+    )(dq, dkv.reshape(2, planes, team, rows, HD))
 
 
 def local_planes(queries, key_states, value_states, outputs, out_grad, doc_of_tile, tile_position):

time: 80.5 us -> 82.4 us (1.024)
  Pallas kernels: 77.3 us -> 78.6 us
    pallas_call x1, Pallas kernels: 15.7 us -> 22.4 us  [attention_backward(): pl.pallas_call(functools.partial(attention_kernel, heads, tiles, team), o...]
    pallas_call x1, Pallas kernels: 30.7 us -> 25.2 us  [give_back(): pl.pallas_call(functools.partial(return_kernel, team, planes), out_shape=...]
where the time goes in v2:
time: 82.4 us; the launch traced here: 80.9 us
  Pallas kernels  78.6 us (95%)
  local copies, waits for them, and re-layouts  1.69 us (2%)
    pallas_call x1, Pallas kernels, bring(): pl.pallas_call(functools.partial(bring_kernel, team, planes), out_shape=(...  30.9 us
    pallas_call x1, Pallas kernels, give_back(): pl.pallas_call(functools.partial(return_kernel, team, planes), out_shape=...  25.2 us
    pallas_call x1, Pallas kernels, attention_backward(): pl.pallas_call(functools.partial(attention_kernel, heads, tiles, team), o...  22.4 us

profile of v2, /device:TPU:15, one launch (start us, length us, event | category | flops | bytes accessed | tf_op | source)
XLA Modules:
  0.0 80.9 jit_solution(17224712448281047704)
XLA Ops:
  0.6 30.9 %shard_map.94 = (bf16[1024,512]{1,0:T(8,128)(2,1)}, bf16[1024,512]{1,0:T(8,128)(2,1)}, f32[8,1,512]{2,1,0:T(1,128)}, bf16[2,4096,128]{2,1,0:T(8,128)(2,1)}) custom-call(bf16[128,4096]{1,0:T(8,128)(2,1)} %q_ref.1, bf16[128,4096]{1,0:T(8,128)(2,1)} %g_ref.1, bf16[128,512]{1,0:T(8,128)(2,1)} %k_ref.1, bf16[128,512]{1,0:T(8,128)(2,1)} %v_ref.1, ...), custom_call_target="tpu_custom_call" | custom-call | bytes 62914560 | tf_op jit(solution)/shard_map/pallas_call | solution.py:597
  31.6 22.4 %shard_map.95 = (bf16[1024,512]{1,0:T(8,128)(2,1)}, bf16[2,4096,128]{2,1,0:T(8,128)(2,1)}) custom-call(s32[32]{0:T(128)} %position_ref.1, s32[32]{0:T(128)} %doc_ref.1, bf16[8,128,512]{2,1,0:T(8,128)(2,1)} %bitcast.8, bf16[8,128,512]{2,1,0:T(8,128)(2,1)} %bitcast.9, f32[8,1,512]{2,1,0:T(1,128)} %get-tuple-element.13.delta_hbm, ...), custom_call_target="tpu_custom_call" | custom-call | flops 6442450944 | bytes 12582912 | tf_op jit(solution)/shard_map/pallas_call | solution.py:308
  54.0 25.2 %shard_map.96 = (bf16[128,4096]{1,0:T(8,128)(2,1)S(1)}, bf16[2,128,512]{2,1,0:T(8,128)(2,1)S(1)}) custom-call(bf16[1024,512]{1,0:T(8,128)(2,1)} %get-tuple-element.15.dq_ref, bf16[2,4,8,128,128]{4,3,2,1,0:T(8,128)(2,1)} %bitcast.7), custom_call_target="tpu_custom_call" | custom-call | bytes 62914560 | tf_op jit(solution)/shard_map/pallas_call | solution.py:832
  79.2 0.7 slice_bitcast_fusion
  79.9 1.0 %copy.11 = bf16[128,4096]{1,0:T(8,128)(2,1)} copy(bf16[128,4096]{1,0:T(8,128)(2,1)S(1)} %get-tuple-element.24) | data formatting | bytes 2097152

commit v3 on v2

--- a/solution.py
+++ b/solution.py
@@ -257,7 +257,7 @@
         add(index, low_a, grad_a)
         combine(index + 1, scores_b, low_b, grad_b)
 
-    turns = (items + 2) // 2
+    turns = (items + 1) // 2
 
     @pl.loop(0, turns // DEEP)
     def _(step):
@@ -267,6 +267,10 @@
     @pl.loop(turns // DEEP * DEEP, turns)
     def _(step):
         add_two(2 * step)
+
+    @pl.when(items % 2 == 0)
+    def _():
+        add(items - 1, low_b, grad_b)
 
     outs = [pltpu.make_async_copy(dkv_own.at[w], dkv_ref.at[w], sems.at[w]) for w in range(2)]
     for which in range(2):
@@ -298,8 +302,7 @@
     tiles = rows // TILE
     count = tokens // TILE
     longest = count // 2
-    most = sum((longest - i + 1) // 2 for i in range(min(tiles, longest)))
-    most = max(most, tiles) + 4
+    most = sum(max(longest - i // 2 + 1, 2) // 2 for i in range(tiles)) + 4
     pair = SPAN * TILE
     smem = pl.BlockSpec(memory_space=pltpu.SMEM)
     hbm = pl.BlockSpec(memory_space=pl.ANY)

time: 82.4 us -> 82.2 us (level)
  the two profiles are of different devices: /device:TPU:15 before, /device:TPU:9 now
where the time goes in v3:
time: 82.2 us; the launch traced here: 80.7 us
  Pallas kernels  78.4 us (95%)
  local copies, waits for them, and re-layouts  1.69 us (2%)
    pallas_call x1, Pallas kernels, bring(): pl.pallas_call(functools.partial(bring_kernel, team, planes), out_shape=(...  31.4 us
    pallas_call x1, Pallas kernels, give_back(): pl.pallas_call(functools.partial(return_kernel, team, planes), out_shape=...  30.6 us
    pallas_call x1, Pallas kernels, attention_backward(): pl.pallas_call(functools.partial(attention_kernel, heads, tiles, team), o...  16.4 us

profile of v3, /device:TPU:9, one launch (start us, length us, event | category | flops | bytes accessed | tf_op | source)
XLA Modules:
  0.0 80.7 jit_solution(1069444377029303823)
XLA Ops:
  0.6 31.4 %shard_map.94 = (bf16[1024,512]{1,0:T(8,128)(2,1)}, bf16[1024,512]{1,0:T(8,128)(2,1)}, f32[8,1,512]{2,1,0:T(1,128)}, bf16[2,4096,128]{2,1,0:T(8,128)(2,1)}) custom-call(bf16[128,4096]{1,0:T(8,128)(2,1)} %q_ref.1, bf16[128,4096]{1,0:T(8,128)(2,1)} %g_ref.1, bf16[128,512]{1,0:T(8,128)(2,1)} %k_ref.1, bf16[128,512]{1,0:T(8,128)(2,1)} %v_ref.1, ...), custom_call_target="tpu_custom_call" | custom-call | bytes 62914560 | tf_op jit(solution)/shard_map/pallas_call | solution.py:600
  32.1 16.4 %shard_map.95 = (bf16[1024,512]{1,0:T(8,128)(2,1)}, bf16[2,4096,128]{2,1,0:T(8,128)(2,1)}) custom-call(s32[32]{0:T(128)} %position_ref.1, s32[32]{0:T(128)} %doc_ref.1, bf16[8,128,512]{2,1,0:T(8,128)(2,1)} %bitcast.8, bf16[8,128,512]{2,1,0:T(8,128)(2,1)} %bitcast.9, f32[8,1,512]{2,1,0:T(1,128)} %get-tuple-element.13.delta_hbm, ...), custom_call_target="tpu_custom_call" | custom-call | flops 6442450944 | bytes 12582912 | tf_op jit(solution)/shard_map/pallas_call | solution.py:311
  48.4 30.6 %shard_map.96 = (bf16[128,4096]{1,0:T(8,128)(2,1)S(1)}, bf16[2,128,512]{2,1,0:T(8,128)(2,1)S(1)}) custom-call(bf16[1024,512]{1,0:T(8,128)(2,1)} %get-tuple-element.15.dq_ref, bf16[2,4,8,128,128]{4,3,2,1,0:T(8,128)(2,1)} %bitcast.7), custom_call_target="tpu_custom_call" | custom-call | bytes 62914560 | tf_op jit(solution)/shard_map/pallas_call | solution.py:835
  79.0 0.7 slice_bitcast_fusion
  79.8 1.0 %copy.11 = bf16[128,4096]{1,0:T(8,128)(2,1)} copy(bf16[128,4096]{1,0:T(8,128)(2,1)S(1)} %get-tuple-element.24) | data formatting | bytes 2097152

commit v4 on v3

--- a/solution.py
+++ b/solution.py
@@ -450,13 +450,16 @@
     for copy in locals_:
         copy.start()
     rest = []
-    for kind, (src, dst) in enumerate(((q_ref, q_out), (g_ref, g_out))):
+
+    def spread(kind, source, dst):
         for shift in range(1, team):
             other = (slot + shift) % team
             lanes = pl.ds(pl.multiple_of(other * width, HD), width)
-            copy = flat(1 + kind, shift, src.at[:, lanes], dst.at[tall, :])
+            copy = flat(kind, shift, source.at[:, lanes], dst.at[tall, :])
             copy.start()
             rest.append(copy)
+
+    spread(1, q_ref, q_out)
     locals_[0].wait()
     part_rows = span // SUB
     per_part = team // SUB
@@ -522,6 +525,8 @@
             chain(1, 0, plane, sub).start()
 
         share(0, plane, sub).start()
+        if sub == 0:
+            spread(2, g_ref, g_out)
 
     loads[2].wait()
     loads[3].wait()

time: 82.2 us -> 80 us (0.973)
  the two profiles are of different devices: /device:TPU:9 before, /device:TPU:15 now
where the time goes in v4:
time: 80 us; the launch traced here: 79.8 us
  Pallas kernels  77.4 us (97%)
  local copies, waits for them, and re-layouts  1.69 us (2%)
    pallas_call x1, Pallas kernels, bring(): pl.pallas_call(functools.partial(bring_kernel, team, planes), out_shape=(...  30.9 us
    pallas_call x1, Pallas kernels, give_back(): pl.pallas_call(functools.partial(return_kernel, team, planes), out_shape=...  30.5 us
    pallas_call x1, Pallas kernels, attention_backward(): pl.pallas_call(functools.partial(attention_kernel, heads, tiles, team), o...  16 us

profile of v4, /device:TPU:15, one launch (start us, length us, event | category | flops | bytes accessed | tf_op | source)
XLA Modules:
  0.0 79.8 jit_solution(9981794517636039416)
XLA Ops:
  0.6 30.9 %shard_map.94 = (bf16[1024,512]{1,0:T(8,128)(2,1)}, bf16[1024,512]{1,0:T(8,128)(2,1)}, f32[8,1,512]{2,1,0:T(1,128)}, bf16[2,4096,128]{2,1,0:T(8,128)(2,1)}) custom-call(bf16[128,4096]{1,0:T(8,128)(2,1)} %q_ref.1, bf16[128,4096]{1,0:T(8,128)(2,1)} %g_ref.1, bf16[128,512]{1,0:T(8,128)(2,1)} %k_ref.1, bf16[128,512]{1,0:T(8,128)(2,1)} %v_ref.1, ...), custom_call_target="tpu_custom_call" | custom-call | bytes 62914560 | tf_op jit(solution)/shard_map/pallas_call | solution.py:605
  31.6 16.0 %shard_map.95 = (bf16[1024,512]{1,0:T(8,128)(2,1)}, bf16[2,4096,128]{2,1,0:T(8,128)(2,1)}) custom-call(s32[32]{0:T(128)} %position_ref.1, s32[32]{0:T(128)} %doc_ref.1, bf16[8,128,512]{2,1,0:T(8,128)(2,1)} %bitcast.8, bf16[8,128,512]{2,1,0:T(8,128)(2,1)} %bitcast.9, f32[8,1,512]{2,1,0:T(1,128)} %get-tuple-element.13.delta_hbm, ...), custom_call_target="tpu_custom_call" | custom-call | flops 6442450944 | bytes 12582912 | tf_op jit(solution)/shard_map/pallas_call | solution.py:311
  47.6 30.5 %shard_map.96 = (bf16[128,4096]{1,0:T(8,128)(2,1)S(1)}, bf16[2,128,512]{2,1,0:T(8,128)(2,1)S(1)}) custom-call(bf16[1024,512]{1,0:T(8,128)(2,1)} %get-tuple-element.15.dq_ref, bf16[2,4,8,128,128]{4,3,2,1,0:T(8,128)(2,1)} %bitcast.7), custom_call_target="tpu_custom_call" | custom-call | bytes 62914560 | tf_op jit(solution)/shard_map/pallas_call | solution.py:840
  78.1 0.7 slice_bitcast_fusion
  78.8 1.0 %copy.11 = bf16[128,4096]{1,0:T(8,128)(2,1)} copy(bf16[128,4096]{1,0:T(8,128)(2,1)S(1)} %get-tuple-element.24) | data formatting | bytes 2097152
